TPU v7x, 256 devices: a whole 4x4x8 slice. The times are simulated.
256 devices in a mesh: batch: 8 (over y, core), proto: 32 (over x, z).
Axes of the slice: x: 4, y: 4, z: 8, core: 2. Of those that a mesh axis runs over, the one named last changes fastest.
Arguments:
- features: bfloat16 [8192, 256], P(('batch', 'proto')), may hold values from -8 to 8
- head_weight: bfloat16 [256, 65536], P('batch', 'proto'), may hold values from -0.375 to 0.375
- student_scores: bfloat16 [2, 8192, 65536], P(None, 'batch', 'proto'), may hold values from -1 to 1
Outputs:
- targets: bfloat16 [8192, 65536], P('batch', 'proto')
- row_loss: float32 [2, 8192], P(None, 'batch')
All inputs are finite; a program needn't handle non-finite values.
Results may differ from a plain program's by a relative error of at most 0.0013.
Values may be sent and summed in bfloat16 or wider, within the bound.
A program may use at most 64 MiB of HBM per device.

v0:
```python
import jax
import jax.numpy as jnp
from jax import lax
from jax.sharding import PartitionSpec as P

PROTOS = 65536
ITERS = 3


TEACHER_TEMP = 0.07
STUDENT_TEMP = 0.1


def normalize_columns(balance):
    column_sum = lax.psum(jnp.sum(balance, axis=0), "batch")
    return balance / column_sum[None, :]


def crop_totals(balance):
    return lax.psum(jnp.sum(balance, axis=1), "proto")


def local(features, head_weight, student_scores):
    gathered = lax.all_gather(features, "proto", axis=0, tiled=True)
    feat_wide = gathered.astype(jnp.float32)
    fnorm = jnp.sqrt(jnp.sum(feat_wide * feat_wide, axis=1) + 1e-06)
    piece = lax.all_gather(head_weight, "batch", axis=0, tiled=True)
    piece_wide = piece.astype(jnp.float32)
    raw = jnp.dot(gathered, piece, preferred_element_type=jnp.float32)
    squares = jnp.sum(piece_wide * piece_wide, axis=0)
    wnorm = jnp.sqrt(squares + 1e-06)
    balance = jnp.exp(raw / (fnorm[:, None] * wnorm[None, :]) / TEACHER_TEMP)
    logits = student_scores.astype(jnp.float32) / STUDENT_TEMP
    exp_sums = jnp.sum(jnp.exp(logits), axis=2)
    for step in range(ITERS - 1):
        balance = normalize_columns(balance)
        balance = balance / crop_totals(balance)[:, None]
    balance = normalize_columns(balance)
    balance = balance / crop_totals(balance)[:, None]
    weighted = jnp.sum(logits * balance[None, :, :], axis=2)
    total_exp, total_weighted = lax.psum((exp_sums, weighted), "proto")
    row_loss = jnp.log(total_exp) - total_weighted
    targets = (balance * PROTOS).astype(jnp.bfloat16)
    return (targets, row_loss)


def solution(mesh):
    return jax.shard_map(
        local,
        mesh=mesh,
        in_specs=(P(("batch", "proto"), None), P("batch", "proto"), P(None, "batch", "proto")),
        out_specs=(P("batch", "proto"), P(None, "batch")),
        check_vma=False,
    )
```

profile of v0, /device:TPU:0, one launch (start us, length us, event | category | flops | bytes accessed | tf_op | source)
XLA Modules:
  0.0 499.8 jit_solution(12925280710833799750)
XLA Ops:
  7.2 0.0 all-gather.2.cloned.1.call-start
  7.2 0.7 all-gather.2.cloned.1.call-update
  7.9 50.8 %all_gather.6 = bf16[1024,256]{1,0:T(8,128)(2,1)S(1)} all-gather(bf16[32,256]{1,0:T(8,128)(2,1)} %param.3), channel_id=1, replica_groups=mesh['batch'=8,'proto'=32] {'proto'}, dimensions={0}, use_global_device_ids=true | all-gather | bytes 540672 | tf_op jit(solution)/shard_map/all_gather | solution.py:24
  58.7 0.2 multiply_reduce_fusion.1
  58.9 0.0 all-gather.2.cloned.1.call-done
  58.9 1.5 multiply_reduce_fusion
  60.4 6.0 %fusion.14 = (f32[2048]{0:T(1024)S(1)}, f32[1024,2048]{1,0:T(8,128)}) fusion(f32[2048]{0:T(1024)S(1)} %add_sqrt_fusion, f32[1024]{0:T(1024)S(1)} %add_sqrt_fusion.1, bf16[1024,256]{1,0:T(8,128)(2,1)S(1)} %all_gather.6, bf16[256,2048]{1,0:T(8,128)(2,1)} %all-gather.2.cloned.1.call-done), kind=kOutput, calls=%fused_computation.27 | convolution fusion | flops 1082128384 | bytes 9981952 | tf_op jit(solution)/shard_map/dot_general | solution.py:29
  66.4 12.6 %psum.56 = f32[2048]{0:T(1024)S(1)} all-reduce(f32[2048]{0:T(1024)S(1)} %get-tuple-element.8), channel_id=1, replica_groups=mesh['batch'=8,'proto'=32] {'batch'}, use_global_device_ids=true, to_apply=%region_3.0 | all-reduce | flops 2048 | bytes 16384 | tf_op jit(solution)/shard_map/psum | solution.py:15
  79.0 4.0 divide_reduce_fusion
  83.0 72.4 %psum.57 = f32[1024]{0:T(1024)S(1)} all-reduce(f32[1024]{0:T(1024)S(1)} %divide_reduce_fusion), channel_id=1, replica_groups=mesh['batch'=8,'proto'=32] {'proto'}, use_global_device_ids=true, to_apply=%region_5.0 | all-reduce | flops 1024 | bytes 8192 | tf_op jit(solution)/shard_map/psum | solution.py:20
  155.4 4.2 fusion.10
  159.6 12.7 %psum.58 = f32[2048]{0:T(1024)S(1)} all-reduce(f32[2048]{0:T(1024)S(1)} %fusion.10), channel_id=1, replica_groups=mesh['batch'=8,'proto'=32] {'batch'}, use_global_device_ids=true, to_apply=%region_7.0 | all-reduce | flops 2048 | bytes 16384 | tf_op jit(solution)/shard_map/psum | solution.py:15
  172.3 4.4 fusion.11
  176.6 69.6 %psum.59 = f32[1024]{0:T(1024)S(1)} all-reduce(f32[1024]{0:T(1024)S(1)} %fusion.11), channel_id=1, replica_groups=mesh['batch'=8,'proto'=32] {'proto'}, use_global_device_ids=true, to_apply=%region_9.0 | all-reduce | flops 1024 | bytes 8192 | tf_op jit(solution)/shard_map/psum | solution.py:20
  246.3 4.5 fusion.12
  250.8 12.7 %psum.60 = f32[2048]{0:T(1024)S(1)} all-reduce(f32[2048]{0:T(1024)S(1)} %fusion.12), channel_id=1, replica_groups=mesh['batch'=8,'proto'=32] {'batch'}, use_global_device_ids=true, to_apply=%region_11.0 | all-reduce | flops 2048 | bytes 16384 | tf_op jit(solution)/shard_map/psum | solution.py:15
  263.5 4.7 fusion.13
  268.1 71.6 %psum.61 = f32[1024]{0:T(1024)S(1)} all-reduce(f32[1024]{0:T(1024)S(1)} %fusion.13), channel_id=1, replica_groups=mesh['batch'=8,'proto'=32] {'proto'}, use_global_device_ids=true, to_apply=%region_13.0 | all-reduce | flops 1024 | bytes 8192 | tf_op jit(solution)/shard_map/psum | solution.py:20
  339.8 6.7 %broadcast_multiply_fusion = (f32[1024,2048]{1,0:T(8,128)S(1)}, bf16[1024,2048]{1,0:T(8,128)(2,1)}) fusion(f32[1024,2048]{1,0:T(8,128)} %get-tuple-element.9, f32[1024]{0:T(1024)S(1)} %psum.61, f32[2048]{0:T(1024)S(1)} %psum.60, f32[1024]{0:T(1024)S(1)} %psum.59, f32[2048]{0:T(1024)S(1)} %psum.58, f32[1024]{0:T(1024)S(1)} %psum.57, f32[2048]{0:T(1024)S(1)} %psum.56), kind=kLoop, calls=%fused_computation.21 | loop fusion | flops 18874368 | bytes 21008384 | tf_op jit(solution)/shard_map/mul | solution.py:40
  346.5 8.1 %fusion.1 = (f32[2,1024]{1,0:T(2,128)S(1)}, f32[2,1024]{1,0:T(2,128)S(1)}) fusion(bf16[2,1024,2048]{2,1,0:T(8,128)(2,1)} %param.5, f32[1024,2048]{1,0:T(8,128)S(1)} %get-tuple-element.6), kind=kLoop, calls=%fused_computation.3 | loop fusion | flops 20967424 | bytes 16793600 | tf_op jit(solution)/shard_map/reduce_sum | solution.py:34
  354.6 137.7 %all-reduce = (f32[2,1024]{1,0:T(2,128)S(1)}, f32[2,1024]{1,0:T(2,128)S(1)}) all-reduce(f32[2,1024]{1,0:T(2,128)S(1)} %get-tuple-element.3, f32[2,1024]{1,0:T(2,128)S(1)} %get-tuple-element.2), channel_id=1, replica_groups=mesh['batch'=8,'proto'=32] {'proto'}, use_global_device_ids=true, to_apply=%region_17.0 | all-reduce | flops 4096 | bytes 32768 | tf_op jit(solution)/shard_map/psum | solution.py:41
  492.3 0.6 log_subtract_fusion
  (2 shorter events, 0.0 us)
Async XLA Ops:
  7.2 51.8 %all-gather.2.cloned.1.call-start = ((), (), s32[]{:S(2)}) async-start(), calls=%async_computation | async-start | bytes 1179648 | tf_op jit(solution)/shard_map/all_gather | solution.py:27
Sparse Core Ops, SparseCore 0:
  9.9 27.1 all-gather.1
where the time goes:
time: 500 us
  blocking collectives  440 us (88%)
  other arithmetic  38.9 us (8%)
  between operations  14.1 us (3%)
  matrix products  5.96 us (1%)
    psum x3, blocking collectives, crop_totals(): return lax.psum(jnp.sum(balance, axis=1), 'proto')  214 us
    psum x1, blocking collectives, local(): total_exp, total_weighted = lax.psum((exp_sums, weighted), 'proto')  138 us
    all_gather x1, blocking collectives, local(): gathered = lax.all_gather(features, 'proto', axis=0, tiled=True)  50.8 us
    psum x3, blocking collectives, normalize_columns(): column_sum = lax.psum(jnp.sum(balance, axis=0), 'batch')  38 us
    reduce_sum x3, other arithmetic, crop_totals(): return lax.psum(jnp.sum(balance, axis=1), 'proto')  13 us
  transfers between devices with their start and end apart: 1, of which 0 were waited for; matrix products, arithmetic and copies ran while one was open for 0% of the time, Pallas kernels for 0%

commit v1 on v0

v1 whole, which is shorter than its diff:
```python
import functools
import math

import jax
import jax.numpy as jnp
from jax import lax
from jax.experimental import pallas as pl
from jax.experimental.pallas import tpu as pltpu
from jax.sharding import PartitionSpec as P

PROTOS = 65536
ITERS = 3
TEACHER_TEMP = 0.07
STUDENT_TEMP = 0.1
LOG2E = math.log2(math.e)

MESH = pl.DeviceIdType.MESH
F32 = jnp.float32
BF16 = jnp.bfloat16
NX, NY, NZ, NC = 4, 4, 8, 2
NB, NP = NY * NC, NX * NZ
ROWS, COLS, DEPTH, VIEWS = 1024, 2048, 256, 2
RB, CB = ROWS // 128, COLS // 128
FCH, WCH = ROWS // NP, DEPTH // NB
STU_CHUNKS = 8


def ring(d, n):
    return min(d, n - d)


BATCH_PEERS = sorted(
    [(dy, dc) for dy in range(NY) for dc in range(NC) if (dy, dc) != (0, 0)],
    key=lambda d: -ring(d[0], NY),
)
PROTO_PEERS = sorted(
    [(dx, dz) for dx in range(NX) for dz in range(NZ) if (dx, dz) != (0, 0)],
    key=lambda d: -(ring(d[0], NX) + ring(d[1], NZ)),
)
Z_NEAR = (1, 7, 2, 6, 3, 5, 4)
X_NEAR = (2, 1, 3)
Y_NEAR = (2, 1, 3)


def tile_cols(piece):
    return jnp.concatenate([piece] * CB, axis=1)


def kernel(
    feat_ref, head_ref, stu_hbm,
    out, loss_ref,
    feat, head, stu, balance, r_rep, part, wide, colacc, inv_w,
    col_buf, row_buf, exp_buf, dot_buf,
    own_sem, stu_sem, f_send, fz_recv, fx_recv, w_send, wy_recv, wc_recv,
    col_send, col_recv, row_send, row_recv, loss_send, loss_recv,
):
    b, p = lax.axis_index("batch"), lax.axis_index("proto")
    y, core = lax.div(b, NC), lax.rem(b, NC)
    x, z = lax.div(p, NZ), lax.rem(p, NZ)

    def batch_at(dy, dc):
        return (lax.rem(y + dy, NY) * NC + lax.rem(core + dc, NC), p)

    def proto_at(dx, dz):
        return (b, lax.rem(x + dx, NX) * NZ + lax.rem(z + dz, NZ))

    def remote(src, dst, send, recv, device):
        copy = pltpu.make_async_remote_copy(
            src_ref=src, dst_ref=dst, send_sem=send, recv_sem=recv, device_id=device, device_id_type=MESH
        )
        copy.start()

    def await_bytes(ref, sem):
        pltpu.make_async_copy(ref, ref, sem).wait()

    def feat_rows(xx, zz):
        return feat.at[pl.ds(pl.multiple_of((xx * NZ + zz) * FCH, FCH), FCH), :]

    def head_rows(yy, cc):
        return head.at[pl.ds(pl.multiple_of((yy * NC + cc) * WCH, WCH), WCH), :]

    own_f, own_w = feat_rows(x, z), head_rows(y, core)
    own_in = [
        pltpu.make_async_copy(feat_ref, own_f, own_sem.at[0]),
        pltpu.make_async_copy(head_ref, own_w, own_sem.at[1]),
    ]
    for copy in own_in:
        copy.start()

    chunk = ROWS // STU_CHUNKS
    scores_in = [
        pltpu.make_async_copy(
            stu_hbm.at[:, pl.ds(k * chunk, chunk), :], stu.at[:, pl.ds(k * chunk, chunk), :], stu_sem.at[k]
        )
        for k in range(STU_CHUNKS)
    ]
    for copy in scores_in:
        copy.start()

    barrier = pltpu.get_barrier_semaphore()
    greeted = [batch_at(*d) for d in BATCH_PEERS]
    greeted += [proto_at(0, dz) for dz in range(1, NZ)] + [proto_at(dx, 0) for dx in range(1, NX)]
    for device in greeted:
        pl.semaphore_signal(barrier, inc=1, device_id=device, device_id_type=MESH)

    for k in range(STU_CHUNKS):
        scores_in[k].wait()

        def exp_rows(i, carry, k=k):
            for v in range(VIEWS):
                row = pl.multiple_of(k * chunk + i * 16, 16)
                e = jnp.exp2(stu[v, pl.ds(row, 16), :].astype(F32) * (LOG2E / STUDENT_TEMP))
                acc = e[:, :128]
                for c in range(1, CB):
                    acc = acc + e[:, c * 128 : (c + 1) * 128]
                wide[v, pl.ds(row, 16), :] = acc
            return carry

        lax.fori_loop(0, chunk // 16, exp_rows, 0)

    pl.semaphore_wait(barrier, len(greeted))

    for copy in own_in:
        copy.wait()
    for i, dz in enumerate(Z_NEAR):
        remote(own_f, own_f, f_send, fz_recv.at[i], proto_at(0, dz))
    for i, dy in enumerate(Y_NEAR):
        remote(own_w, own_w, w_send, wy_recv.at[i], batch_at(dy, 0))
    for i, dx in enumerate(X_NEAR):
        remote(own_f, own_f, f_send, fx_recv.at[i], proto_at(dx, 0))
    remote(own_w, own_w, w_send, wc_recv, batch_at(0, 1))
    for i, dz in enumerate(Z_NEAR):
        piece = feat_rows(x, lax.rem(z + NZ - dz, NZ))
        await_bytes(piece, fz_recv.at[i])
        for j, dx in enumerate(X_NEAR):
            remote(piece, piece, f_send, fx_recv.at[j], proto_at(dx, 0))
    for i in (1, 2, 0):
        piece = head_rows(lax.rem(y + NY - Y_NEAR[i], NY), core)
        await_bytes(piece, wy_recv.at[i])
        remote(piece, piece, w_send, wc_recv, batch_at(0, 1))
    await_bytes(head.at[pl.ds(0, NY * WCH), :], wc_recv)

    for c in range(4):
        cols = pl.ds(c * 512, 512)
        w_wide = head[:, cols].astype(F32)
        inv_w[:, cols] = 1.0 / jnp.sqrt(jnp.sum(w_wide * w_wide, axis=0, keepdims=True) + 1e-06)
    colacc[...] = jnp.zeros_like(colacc)

    def fill(block):
        first = pl.multiple_of(block * (NZ * FCH), NZ * FCH)
        f_wide = feat[pl.ds(first, 256), :].astype(F32)
        inv_f = (LOG2E / TEACHER_TEMP) / jnp.sqrt(jnp.sum(f_wide * f_wide, axis=1, keepdims=True) + 1e-06)

        def columns(c, carry):
            cols = pl.ds(pl.multiple_of(c * 256, 256), 256)
            raw = jnp.dot(feat[pl.ds(first, 256), :], head[:, cols], preferred_element_type=F32)
            e = jnp.exp2(raw * inv_f * inv_w[:, cols])
            balance[pl.ds(first, 256), cols] = e
            colacc[:, cols] += jnp.sum(e.reshape(32, 8, 256), axis=0)
            return carry

        lax.fori_loop(0, COLS // 256, columns, 0)

    fill(x)
    for j in (1, 2, 0):
        block = lax.rem(x + NX - X_NEAR[j], NX)
        await_bytes(feat.at[pl.ds(pl.multiple_of(block * 256, 256), 256), :], fx_recv.at[j])
        fill(block)

    def lane_sums(get):
        return jnp.concatenate(
            [jnp.sum(get(a).T, axis=0, keepdims=True) for a in range(RB)], axis=0
        )

    def send_rows(mine, buf_of, send, recv):
        for dx, dz in PROTO_PEERS:
            remote(mine, mine, send, recv, proto_at(dx, dz))

    def total(buf, n):
        acc = buf[0]
        for k in range(1, n):
            acc = acc + buf[k]
        return acc

    for step in range(ITERS):
        if step > 0:

            def col_rows(i, acc):
                for u in range(4):
                    row = pl.multiple_of(i * 32 + u * 8, 8)
                    acc = acc + balance[pl.ds(row, 8), :] * tile_cols(r_rep[pl.ds(row, 8), :])
                return acc

            colacc[...] = lax.fori_loop(0, ROWS // 32, col_rows, jnp.zeros((8, COLS), F32))
        sums = jnp.sum(colacc[...], axis=0, keepdims=True)
        mine = col_buf.at[step, b]
        for k in range(CB):
            mine[k : k + 1, :] = sums[:, k * 128 : (k + 1) * 128]
        for dy, dc in BATCH_PEERS:
            remote(mine, mine, col_send.at[step], col_recv.at[step], batch_at(dy, dc))
        await_bytes(col_buf.at[step, pl.ds(0, NB - 1)], col_recv.at[step])
        col_inv = 1.0 / total(col_buf.at[step], NB)
        col_wide = jnp.concatenate(
            [jnp.broadcast_to(col_inv[k : k + 1, :], (8, 128)) for k in range(CB)], axis=1
        )

        def row_rows(i, carry):
            for u in range(4):
                row = pl.multiple_of(i * 32 + u * 8, 8)
                q = balance[pl.ds(row, 8), :] * col_wide
                acc = q[:, :128]
                for c in range(1, CB):
                    acc = acc + q[:, c * 128 : (c + 1) * 128]
                part[pl.ds(row, 8), :] = acc
            return carry

        lax.fori_loop(0, ROWS // 32, row_rows, 0)
        mine = row_buf.at[step, p]
        mine[...] = lane_sums(lambda a: part[a * 128 : (a + 1) * 128, :])
        send_rows(mine, row_buf, row_send.at[step], row_recv.at[step])
        if step == 0:
            mine = exp_buf.at[p]
            for v in range(VIEWS):
                mine[v] = lane_sums(lambda a: wide[v, a * 128 : (a + 1) * 128, :])
            send_rows(mine, exp_buf, loss_send.at[0], loss_recv.at[0])
        if step == ITERS - 1:

            def dot_rows(i, carry):
                row = pl.multiple_of(i * 16, 16)
                q = balance[pl.ds(row, 16), :] * jnp.concatenate([col_wide, col_wide], axis=0)
                balance[pl.ds(row, 16), :] = q
                for v in range(VIEWS):
                    t = q * stu[v, pl.ds(row, 16), :].astype(F32)
                    acc = t[:, :128]
                    for c in range(1, CB):
                        acc = acc + t[:, c * 128 : (c + 1) * 128]
                    wide[v, pl.ds(row, 16), :] = acc
                return carry

            lax.fori_loop(0, ROWS // 16, dot_rows, 0)
            mine = dot_buf.at[p]
            for v in range(VIEWS):
                mine[v] = lane_sums(lambda a: wide[v, a * 128 : (a + 1) * 128, :])
            send_rows(mine, dot_buf, loss_send.at[1], loss_recv.at[1])
        await_bytes(row_buf.at[step, pl.ds(0, NP - 1)], row_recv.at[step])
        row_inv = 1.0 / total(row_buf.at[step], NP)
        for a in range(RB):
            r_rep[a * 128 : (a + 1) * 128, :] = jnp.broadcast_to(row_inv[a : a + 1, :], (128, 128)).T

    for a in range(RB):

        def out_rows(i, carry, a=a):
            row = pl.multiple_of(a * 128 + i * 16, 16)
            q = balance[pl.ds(row, 16), :] * tile_cols(r_rep[pl.ds(row, 16), :] * float(PROTOS))
            out[pl.ds(row, 16), :] = q.astype(BF16)
            return carry

        lax.fori_loop(0, 8, out_rows, 0)

    await_bytes(exp_buf.at[pl.ds(0, NP - 1)], loss_recv.at[0])
    await_bytes(dot_buf.at[pl.ds(0, NP - 1)], loss_recv.at[1])
    exps, dots = total(exp_buf, NP), total(dot_buf, NP)
    for v in range(VIEWS):
        row_loss = jnp.log(exps[v]) - dots[v] * row_inv * (1.0 / STUDENT_TEMP)
        for a in range(RB):
            loss_ref[v : v + 1, a * 128 : (a + 1) * 128] = row_loss[a : a + 1, :]

    await_bytes(feat.at[pl.ds(0, (NP - 1) * FCH), :], f_send)
    await_bytes(head.at[pl.ds(0, (NB - 1) * WCH), :], w_send)
    for step in range(ITERS):
        await_bytes(col_buf.at[step, pl.ds(0, NB - 1)], col_send.at[step])
        await_bytes(row_buf.at[step, pl.ds(0, NP - 1)], row_send.at[step])
    await_bytes(exp_buf.at[pl.ds(0, NP - 1)], loss_send.at[0])
    await_bytes(dot_buf.at[pl.ds(0, NP - 1)], loss_send.at[1])


def local(features, head_weight, student_scores):
    dma = pltpu.SemaphoreType.DMA
    return pl.pallas_call(
        kernel,
        out_shape=(
            jax.ShapeDtypeStruct((ROWS, COLS), BF16),
            jax.ShapeDtypeStruct((VIEWS, ROWS), F32),
        ),
        in_specs=[
            pl.BlockSpec(memory_space=pltpu.HBM),
            pl.BlockSpec(memory_space=pltpu.HBM),
            pl.BlockSpec(memory_space=pltpu.HBM),
        ],
        out_specs=(pl.BlockSpec(memory_space=pltpu.VMEM), pl.BlockSpec(memory_space=pltpu.VMEM)),
        scratch_shapes=[
            pltpu.VMEM((ROWS, DEPTH), BF16),
            pltpu.VMEM((DEPTH, COLS), BF16),
            pltpu.VMEM((VIEWS, ROWS, COLS), BF16),
            pltpu.VMEM((ROWS, COLS), F32),
            pltpu.VMEM((ROWS, 128), F32),
            pltpu.VMEM((ROWS, 128), F32),
            pltpu.VMEM((VIEWS, ROWS, 128), F32),
            pltpu.VMEM((8, COLS), F32),
            pltpu.VMEM((1, COLS), F32),
            pltpu.VMEM((ITERS, NB, CB, 128), F32),
            pltpu.VMEM((ITERS, NP, RB, 128), F32),
            pltpu.VMEM((NP, VIEWS, RB, 128), F32),
            pltpu.VMEM((NP, VIEWS, RB, 128), F32),
            dma((2,)),
            dma((STU_CHUNKS,)),
            dma,
            dma((NZ - 1,)),
            dma((NX - 1,)),
            dma,
            dma((NY - 1,)),
            dma,
            dma((ITERS,)),
            dma((ITERS,)),
            dma((ITERS,)),
            dma((ITERS,)),
            dma((2,)),
            dma((2,)),
        ],
        compiler_params=pltpu.CompilerParams(
            collective_id=0, has_side_effects=True, vmem_limit_bytes=48 * 1024 * 1024
        ),
    )(features, head_weight, student_scores)


def solution(mesh):
    return jax.shard_map(
        local,
        mesh=mesh,
        in_specs=(P(("batch", "proto"), None), P("batch", "proto"), P(None, "batch", "proto")),
        out_specs=(P("batch", "proto"), P(None, "batch")),
        check_vma=False,
    )
```

time: 500 us -> 75.1 us (0.15)
  the two profiles are of different devices: /device:TPU:0 before, /device:TPU:1 now
where the time goes in v1:
time: 75.1 us; the launch traced here: 74.9 us
  Pallas kernels  70.1 us (93%)
  local copies, waits for them, and re-layouts  4.23 us (6%)
    pallas_call x1, Pallas kernels, local(): pl.pallas_call(kernel, out_shape=(jax.ShapeDtypeStruct((ROWS, COLS), BF16...  70.1 us
    unnamed x6, local copies, waits for them, and re-layouts  4.23 us

profile of v1, /device:TPU:1, one launch (start us, length us, event | category | flops | bytes accessed | tf_op | source)
XLA Modules:
  0.0 74.9 jit_solution(1767431672960632058)
XLA Ops:
  0.6 0.0 copy-start
  0.6 0.9 %copy-done = bf16[32,2048]{1,0:T(8,128)(2,1)S(1)} copy-done((bf16[32,2048]{1,0:T(8,128)(2,1)S(1)}, bf16[32,2048]{1,0:T(8,128)(2,1)}, u32[]{:S(2)}) %copy-start) | copy-done | bytes 131096
  1.5 0.0 copy-start.1
  1.5 0.7 copy-done.1
  2.3 70.1 %shard_map.50 = (bf16[1024,2048]{1,0:T(8,128)(2,1)S(1)}, f32[2,1024]{1,0:T(2,128)S(1)}) custom-call(bf16[32,256]{1,0:T(8,128)(2,1)S(1)} %copy-done.1, bf16[32,2048]{1,0:T(8,128)(2,1)S(1)} %copy-done, bf16[2,1024,2048]{2,1,0:T(8,128)(2,1)} %stu_hbm.1), custom_call_target="tpu_custom_call" | custom-call | tf_op jit(solution)/shard_map/pallas_call | solution.py:279
  72.3 2.0 %copy.7 = bf16[1024,2048]{1,0:T(8,128)(2,1)} copy(bf16[1024,2048]{1,0:T(8,128)(2,1)S(1)} %get-tuple-element.4) | data formatting | bytes 8388608
  74.3 0.6 copy.8
Async XLA Ops:
  0.6 0.9 %copy-start = (bf16[32,2048]{1,0:T(8,128)(2,1)S(1)}, bf16[32,2048]{1,0:T(8,128)(2,1)}, u32[]{:S(2)}) copy-start(bf16[32,2048]{1,0:T(8,128)(2,1)} %head_ref.1) | copy-start | bytes 393220
  1.5 0.7 copy-start.1

commit v2 on v1

--- a/solution.py
+++ b/solution.py
@@ -23,6 +23,7 @@
 RB, CB = ROWS // 128, COLS // 128
 FCH, WCH = ROWS // NP, DEPTH // NB
 STU_CHUNKS = 8
+VMEM_LIMIT = 48 * 1024 * 1024
 
 
 def ring(d, n):
@@ -46,6 +47,13 @@
     return jnp.concatenate([piece] * CB, axis=1)
 
 
+def fold(wide):
+    tiles = [wide[:, k * 128 : (k + 1) * 128] for k in range(CB)]
+    while len(tiles) > 1:
+        tiles = [tiles[k] + tiles[k + 1] for k in range(0, len(tiles), 2)]
+    return tiles[0]
+
+
 def kernel(
     feat_ref, head_ref, stu_hbm,
     out, loss_ref,
@@ -102,21 +110,6 @@
     greeted += [proto_at(0, dz) for dz in range(1, NZ)] + [proto_at(dx, 0) for dx in range(1, NX)]
     for device in greeted:
         pl.semaphore_signal(barrier, inc=1, device_id=device, device_id_type=MESH)
-
-    for k in range(STU_CHUNKS):
-        scores_in[k].wait()
-
-        def exp_rows(i, carry, k=k):
-            for v in range(VIEWS):
-                row = pl.multiple_of(k * chunk + i * 16, 16)
-                e = jnp.exp2(stu[v, pl.ds(row, 16), :].astype(F32) * (LOG2E / STUDENT_TEMP))
-                acc = e[:, :128]
-                for c in range(1, CB):
-                    acc = acc + e[:, c * 128 : (c + 1) * 128]
-                wide[v, pl.ds(row, 16), :] = acc
-            return carry
-
-        lax.fori_loop(0, chunk // 16, exp_rows, 0)
 
     pl.semaphore_wait(barrier, len(greeted))
 
@@ -151,15 +144,10 @@
         f_wide = feat[pl.ds(first, 256), :].astype(F32)
         inv_f = (LOG2E / TEACHER_TEMP) / jnp.sqrt(jnp.sum(f_wide * f_wide, axis=1, keepdims=True) + 1e-06)
 
-        def columns(c, carry):
-            cols = pl.ds(pl.multiple_of(c * 256, 256), 256)
-            raw = jnp.dot(feat[pl.ds(first, 256), :], head[:, cols], preferred_element_type=F32)
-            e = jnp.exp2(raw * inv_f * inv_w[:, cols])
-            balance[pl.ds(first, 256), cols] = e
-            colacc[:, cols] += jnp.sum(e.reshape(32, 8, 256), axis=0)
-            return carry
-
-        lax.fori_loop(0, COLS // 256, columns, 0)
+        raw = jnp.dot(feat[pl.ds(first, 256), :], head[...], preferred_element_type=F32)
+        e = jnp.exp2(raw * inv_f * inv_w[...])
+        balance[pl.ds(first, 256), :] = e
+        colacc[...] += jnp.sum(e.reshape(32, 8, COLS), axis=0)
 
     fill(x)
     for j in (1, 2, 0):
@@ -167,6 +155,19 @@
         await_bytes(feat.at[pl.ds(pl.multiple_of(block * 256, 256), 256), :], fx_recv.at[j])
         fill(block)
 
+    def exp_sums():
+        for k in range(STU_CHUNKS):
+            scores_in[k].wait()
+
+            def exp_rows(i, carry, k=k):
+                for v in range(VIEWS):
+                    row = pl.multiple_of(k * chunk + i * 16, 16)
+                    e = jnp.exp2(stu[v, pl.ds(row, 16), :].astype(F32) * (LOG2E / STUDENT_TEMP))
+                    wide[v, pl.ds(row, 16), :] = fold(e)
+                return carry
+
+            lax.fori_loop(0, chunk // 16, exp_rows, 0)
+
     def lane_sums(get):
         return jnp.concatenate(
             [jnp.sum(get(a).T, axis=0, keepdims=True) for a in range(RB)], axis=0
@@ -186,12 +187,12 @@
         if step > 0:
 
             def col_rows(i, acc):
-                for u in range(4):
-                    row = pl.multiple_of(i * 32 + u * 8, 8)
+                for u in range(16):
+                    row = pl.multiple_of(i * 128 + u * 8, 8)
                     acc = acc + balance[pl.ds(row, 8), :] * tile_cols(r_rep[pl.ds(row, 8), :])
                 return acc
 
-            colacc[...] = lax.fori_loop(0, ROWS // 32, col_rows, jnp.zeros((8, COLS), F32))
+            colacc[...] = lax.fori_loop(0, ROWS // 128, col_rows, jnp.zeros((8, COLS), F32))
         sums = jnp.sum(colacc[...], axis=0, keepdims=True)
         mine = col_buf.at[step, b]
         for k in range(CB):
@@ -205,65 +206,60 @@
         )
 
         def row_rows(i, carry):
-            for u in range(4):
-                row = pl.multiple_of(i * 32 + u * 8, 8)
-                q = balance[pl.ds(row, 8), :] * col_wide
-                acc = q[:, :128]
-                for c in range(1, CB):
-                    acc = acc + q[:, c * 128 : (c + 1) * 128]
-                part[pl.ds(row, 8), :] = acc
+            for u in range(16):
+                row = pl.multiple_of(i * 128 + u * 8, 8)
+                part[pl.ds(row, 8), :] = fold(balance[pl.ds(row, 8), :] * col_wide)
             return carry
 
-        lax.fori_loop(0, ROWS // 32, row_rows, 0)
+        lax.fori_loop(0, ROWS // 128, row_rows, 0)
         mine = row_buf.at[step, p]
         mine[...] = lane_sums(lambda a: part[a * 128 : (a + 1) * 128, :])
         send_rows(mine, row_buf, row_send.at[step], row_recv.at[step])
         if step == 0:
+            exp_sums()
             mine = exp_buf.at[p]
             for v in range(VIEWS):
                 mine[v] = lane_sums(lambda a: wide[v, a * 128 : (a + 1) * 128, :])
             send_rows(mine, exp_buf, loss_send.at[0], loss_recv.at[0])
         if step == ITERS - 1:
 
-            def dot_rows(i, carry):
-                row = pl.multiple_of(i * 16, 16)
-                q = balance[pl.ds(row, 16), :] * jnp.concatenate([col_wide, col_wide], axis=0)
-                balance[pl.ds(row, 16), :] = q
-                for v in range(VIEWS):
-                    t = q * stu[v, pl.ds(row, 16), :].astype(F32)
-                    acc = t[:, :128]
-                    for c in range(1, CB):
-                        acc = acc + t[:, c * 128 : (c + 1) * 128]
-                    wide[v, pl.ds(row, 16), :] = acc
-                return carry
-
-            lax.fori_loop(0, ROWS // 16, dot_rows, 0)
-            mine = dot_buf.at[p]
             for v in range(VIEWS):
-                mine[v] = lane_sums(lambda a: wide[v, a * 128 : (a + 1) * 128, :])
-            send_rows(mine, dot_buf, loss_send.at[1], loss_recv.at[1])
+
+                def dot_rows(i, carry, v=v):
+                    for u in range(4):
+                        row = pl.multiple_of(i * 64 + u * 16, 16)
+                        q = balance[pl.ds(row, 16), :]
+                        if v == 0:
+                            q = q * jnp.concatenate([col_wide, col_wide], axis=0)
+                            balance[pl.ds(row, 16), :] = q
+                        wide[v, pl.ds(row, 16), :] = fold(q * stu[v, pl.ds(row, 16), :].astype(F32))
+                    return carry
+
+                lax.fori_loop(0, ROWS // 64, dot_rows, 0)
+                mine = dot_buf.at[v, p]
+                mine[...] = lane_sums(lambda a: wide[v, a * 128 : (a + 1) * 128, :])
+                send_rows(mine, dot_buf, loss_send.at[1 + v], loss_recv.at[1 + v])
         await_bytes(row_buf.at[step, pl.ds(0, NP - 1)], row_recv.at[step])
         row_inv = 1.0 / total(row_buf.at[step], NP)
         for a in range(RB):
             r_rep[a * 128 : (a + 1) * 128, :] = jnp.broadcast_to(row_inv[a : a + 1, :], (128, 128)).T
 
-    for a in range(RB):
-
-        def out_rows(i, carry, a=a):
-            row = pl.multiple_of(a * 128 + i * 16, 16)
+    def out_rows(i, carry):
+        for u in range(4):
+            row = pl.multiple_of(i * 64 + u * 16, 16)
             q = balance[pl.ds(row, 16), :] * tile_cols(r_rep[pl.ds(row, 16), :] * float(PROTOS))
             out[pl.ds(row, 16), :] = q.astype(BF16)
-            return carry
-
-        lax.fori_loop(0, 8, out_rows, 0)
+        return carry
+
+    lax.fori_loop(0, ROWS // 64, out_rows, 0)
 
     await_bytes(exp_buf.at[pl.ds(0, NP - 1)], loss_recv.at[0])
-    await_bytes(dot_buf.at[pl.ds(0, NP - 1)], loss_recv.at[1])
-    exps, dots = total(exp_buf, NP), total(dot_buf, NP)
     for v in range(VIEWS):
-        row_loss = jnp.log(exps[v]) - dots[v] * row_inv * (1.0 / STUDENT_TEMP)
-        for a in range(RB):
-            loss_ref[v : v + 1, a * 128 : (a + 1) * 128] = row_loss[a : a + 1, :]
+        await_bytes(dot_buf.at[v, pl.ds(0, NP - 1)], loss_recv.at[1 + v])
+    exps = total(exp_buf, NP)
+    for v in range(VIEWS):
+        row_loss = jnp.log(exps[v]) - total(dot_buf.at[v], NP) * row_inv * (1.0 / STUDENT_TEMP)
+        loss_ref[v] = row_loss
 
     await_bytes(feat.at[pl.ds(0, (NP - 1) * FCH), :], f_send)
     await_bytes(head.at[pl.ds(0, (NB - 1) * WCH), :], w_send)
@@ -271,23 +267,36 @@
         await_bytes(col_buf.at[step, pl.ds(0, NB - 1)], col_send.at[step])
         await_bytes(row_buf.at[step, pl.ds(0, NP - 1)], row_send.at[step])
     await_bytes(exp_buf.at[pl.ds(0, NP - 1)], loss_send.at[0])
-    await_bytes(dot_buf.at[pl.ds(0, NP - 1)], loss_send.at[1])
+    for v in range(VIEWS):
+        await_bytes(dot_buf.at[v, pl.ds(0, NP - 1)], loss_send.at[1 + v])
+
+
+def finish(out, loss_in, tgt_hbm, loss_hbm, loss, sem, loss_sem):
+    copies = []
+    for a in range(RB):
+        rows = pl.ds(a * 128, 128)
+        copies.append(pltpu.make_async_copy(out.at[rows, :], tgt_hbm.at[rows, :], sem.at[a]))
+        copies[-1].start()
+    for v in range(VIEWS):
+        for a in range(RB):
+            loss[v : v + 1, a * 128 : (a + 1) * 128] = loss_in[v, a : a + 1, :]
+    copies.append(pltpu.make_async_copy(loss, loss_hbm, loss_sem))
+    copies[-1].start()
+    for copy in copies:
+        copy.wait()
 
 
 def local(features, head_weight, student_scores):
+    in_vmem, in_hbm = pl.BlockSpec(memory_space=pltpu.VMEM), pl.BlockSpec(memory_space=pltpu.HBM)
     dma = pltpu.SemaphoreType.DMA
-    return pl.pallas_call(
+    out, loss = pl.pallas_call(
         kernel,
         out_shape=(
             jax.ShapeDtypeStruct((ROWS, COLS), BF16),
-            jax.ShapeDtypeStruct((VIEWS, ROWS), F32),
+            jax.ShapeDtypeStruct((VIEWS, RB, 128), F32),
         ),
-        in_specs=[
-            pl.BlockSpec(memory_space=pltpu.HBM),
-            pl.BlockSpec(memory_space=pltpu.HBM),
-            pl.BlockSpec(memory_space=pltpu.HBM),
-        ],
-        out_specs=(pl.BlockSpec(memory_space=pltpu.VMEM), pl.BlockSpec(memory_space=pltpu.VMEM)),
+        in_specs=[in_hbm] * 3,
+        out_specs=(in_vmem,) * 2,
         scratch_shapes=[
             pltpu.VMEM((ROWS, DEPTH), BF16),
             pltpu.VMEM((DEPTH, COLS), BF16),
@@ -301,7 +310,7 @@
             pltpu.VMEM((ITERS, NB, CB, 128), F32),
             pltpu.VMEM((ITERS, NP, RB, 128), F32),
             pltpu.VMEM((NP, VIEWS, RB, 128), F32),
-            pltpu.VMEM((NP, VIEWS, RB, 128), F32),
+            pltpu.VMEM((VIEWS, NP, RB, 128), F32),
             dma((2,)),
             dma((STU_CHUNKS,)),
             dma,
@@ -314,13 +323,28 @@
             dma((ITERS,)),
             dma((ITERS,)),
             dma((ITERS,)),
-            dma((2,)),
-            dma((2,)),
+            dma((1 + VIEWS,)),
+            dma((1 + VIEWS,)),
         ],
         compiler_params=pltpu.CompilerParams(
-            collective_id=0, has_side_effects=True, vmem_limit_bytes=48 * 1024 * 1024
+            collective_id=0, has_side_effects=True, vmem_limit_bytes=VMEM_LIMIT
         ),
-    )(features, head_weight, student_scores)
+    )(*(pltpu.with_memory_space_constraint(a, pltpu.HBM) for a in (features, head_weight, student_scores)))
+    return pl.pallas_call(
+        finish,
+        out_shape=(
+            jax.ShapeDtypeStruct((ROWS, COLS), BF16),
+            jax.ShapeDtypeStruct((VIEWS, ROWS), F32),
+        ),
+        in_specs=[in_vmem] * 2,
+        out_specs=(in_hbm,) * 2,
+        scratch_shapes=[
+            pltpu.VMEM((VIEWS, ROWS), F32),
+            dma((RB,)),
+            dma,
+        ],
+        compiler_params=pltpu.CompilerParams(vmem_limit_bytes=16 * 1024 * 1024),
+    )(out, loss)
 
 
 def solution(mesh):

time: 75.1 us -> 64.5 us (0.86)
  Pallas kernels: 70.1 us -> 63.8 us
  local copies, waits for them, and re-layouts: 4.23 us -> 0 us
    pallas_call x1, Pallas kernels: 70.1 us -> 61.7 us  [local(): pl.pallas_call(kernel, out_shape=(jax.ShapeDtypeStruct((ROWS, COLS), BF16...]
    unnamed x6 -> x0, local copies, waits for them, and re-layouts: 4.23 us -> none
    pallas_call x0 -> x1, Pallas kernels: none -> 2.08 us  [local(): pl.pallas_call(finish, out_shape=(jax.ShapeDtypeStruct((ROWS, COLS), BF16...]
where the time goes in v2:
time: 64.5 us; the launch traced here: 64.4 us
  Pallas kernels  63.8 us (99%)
    pallas_call x1, Pallas kernels, local(): pl.pallas_call(kernel, out_shape=(jax.ShapeDtypeStruct((ROWS, COLS), BF16...  61.7 us
    pallas_call x1, Pallas kernels, local(): pl.pallas_call(finish, out_shape=(jax.ShapeDtypeStruct((ROWS, COLS), BF16...  2.08 us

profile of v2, /device:TPU:1, one launch (start us, length us, event | category | flops | bytes accessed | tf_op | source)
XLA Modules:
  0.0 64.4 jit_solution(3193720191462688618)
XLA Ops:
  0.6 61.7 %shard_map.50 = (bf16[1024,2048]{1,0:T(8,128)(2,1)S(1)}, f32[2,8,128]{2,1,0:T(8,128)S(1)}) custom-call(bf16[32,256]{1,0:T(8,128)(2,1)} %feat_ref.1, bf16[32,2048]{1,0:T(8,128)(2,1)} %head_ref.1, bf16[2,1024,2048]{2,1,0:T(8,128)(2,1)} %stu_hbm.1), custom_call_target="tpu_custom_call" | custom-call | tf_op jit(solution)/shard_map/pallas_call | solution.py:292
  62.3 2.1 %shard_map.51 = (bf16[1024,2048]{1,0:T(8,128)(2,1)}, f32[2,1024]{1,0:T(2,128)}) custom-call(bf16[1024,2048]{1,0:T(8,128)(2,1)S(1)} %get-tuple-element.4.out, f32[2,8,128]{2,1,0:T(8,128)S(1)} %get-tuple-element.5.loss_in), custom_call_target="tpu_custom_call" | custom-call | tf_op jit(solution)/shard_map/pallas_call | solution.py:333

commit v3 on v2

--- a/solution.py
+++ b/solution.py
@@ -102,12 +102,9 @@
         )
         for k in range(STU_CHUNKS)
     ]
-    for copy in scores_in:
-        copy.start()
-
     barrier = pltpu.get_barrier_semaphore()
     greeted = [batch_at(*d) for d in BATCH_PEERS]
-    greeted += [proto_at(0, dz) for dz in range(1, NZ)] + [proto_at(dx, 0) for dx in range(1, NX)]
+    greeted = [proto_at(0, dz) for dz in reversed(Z_NEAR)] + greeted + [proto_at(dx, 0) for dx in range(1, NX)]
     for device in greeted:
         pl.semaphore_signal(barrier, inc=1, device_id=device, device_id_type=MESH)
 
@@ -122,6 +119,8 @@
     for i, dx in enumerate(X_NEAR):
         remote(own_f, own_f, f_send, fx_recv.at[i], proto_at(dx, 0))
     remote(own_w, own_w, w_send, wc_recv, batch_at(0, 1))
+    for copy in scores_in:
+        copy.start()
     for i, dz in enumerate(Z_NEAR):
         piece = feat_rows(x, lax.rem(z + NZ - dz, NZ))
         await_bytes(piece, fz_recv.at[i])
@@ -213,7 +212,8 @@
 
         lax.fori_loop(0, ROWS // 128, row_rows, 0)
         mine = row_buf.at[step, p]
-        mine[...] = lane_sums(lambda a: part[a * 128 : (a + 1) * 128, :])
+        own_sums = lane_sums(lambda a: part[a * 128 : (a + 1) * 128, :])
+        mine[...] = own_sums
         send_rows(mine, row_buf, row_send.at[step], row_recv.at[step])
         if step == 0:
             exp_sums()
@@ -222,23 +222,27 @@
                 mine[v] = lane_sums(lambda a: wide[v, a * 128 : (a + 1) * 128, :])
             send_rows(mine, exp_buf, loss_send.at[0], loss_recv.at[0])
         if step == ITERS - 1:
-
-            for v in range(VIEWS):
-
-                def dot_rows(i, carry, v=v):
-                    for u in range(4):
-                        row = pl.multiple_of(i * 64 + u * 16, 16)
-                        q = balance[pl.ds(row, 16), :]
-                        if v == 0:
-                            q = q * jnp.concatenate([col_wide, col_wide], axis=0)
-                            balance[pl.ds(row, 16), :] = q
+            await_bytes(exp_buf.at[pl.ds(0, NP - 1)], loss_recv.at[0])
+            lse = jnp.log(total(exp_buf, NP))
+
+            def dot_rows(i, carry):
+                for u in range(2):
+                    row = pl.multiple_of(i * 32 + u * 16, 16)
+                    q = balance[pl.ds(row, 16), :] * jnp.concatenate([col_wide, col_wide], axis=0)
+                    balance[pl.ds(row, 16), :] = q
+                    for v in range(VIEWS):
                         wide[v, pl.ds(row, 16), :] = fold(q * stu[v, pl.ds(row, 16), :].astype(F32))
-                    return carry
-
-                lax.fori_loop(0, ROWS // 64, dot_rows, 0)
-                mine = dot_buf.at[v, p]
-                mine[...] = lane_sums(lambda a: wide[v, a * 128 : (a + 1) * 128, :])
-                send_rows(mine, dot_buf, loss_send.at[1 + v], loss_recv.at[1 + v])
+                return carry
+
+            lax.fori_loop(0, ROWS // 32, dot_rows, 0)
+            losses = [
+                lse[v] * own_sums
+                - lane_sums(lambda a: wide[v, a * 128 : (a + 1) * 128, :]) * (1.0 / STUDENT_TEMP)
+                for v in range(VIEWS)
+            ]
+            mine = dot_buf.at[p]
+            mine[...] = jnp.concatenate(losses, axis=0).astype(BF16)
+            send_rows(mine, dot_buf, loss_send.at[1], loss_recv.at[1])
         await_bytes(row_buf.at[step, pl.ds(0, NP - 1)], row_recv.at[step])
         row_inv = 1.0 / total(row_buf.at[step], NP)
         for a in range(RB):
@@ -253,13 +257,12 @@
 
     lax.fori_loop(0, ROWS // 64, out_rows, 0)
 
-    await_bytes(exp_buf.at[pl.ds(0, NP - 1)], loss_recv.at[0])
+    await_bytes(dot_buf.at[pl.ds(0, NP - 1)], loss_recv.at[1])
+    losses = dot_buf[0].astype(F32)
+    for k in range(1, NP):
+        losses = losses + dot_buf[k].astype(F32)
     for v in range(VIEWS):
-        await_bytes(dot_buf.at[v, pl.ds(0, NP - 1)], loss_recv.at[1 + v])
-    exps = total(exp_buf, NP)
-    for v in range(VIEWS):
-        row_loss = jnp.log(exps[v]) - total(dot_buf.at[v], NP) * row_inv * (1.0 / STUDENT_TEMP)
-        loss_ref[v] = row_loss
+        loss_ref[v] = losses[v * RB : (v + 1) * RB, :] * row_inv
 
     await_bytes(feat.at[pl.ds(0, (NP - 1) * FCH), :], f_send)
     await_bytes(head.at[pl.ds(0, (NB - 1) * WCH), :], w_send)
@@ -267,8 +270,7 @@
         await_bytes(col_buf.at[step, pl.ds(0, NB - 1)], col_send.at[step])
         await_bytes(row_buf.at[step, pl.ds(0, NP - 1)], row_send.at[step])
     await_bytes(exp_buf.at[pl.ds(0, NP - 1)], loss_send.at[0])
-    for v in range(VIEWS):
-        await_bytes(dot_buf.at[v, pl.ds(0, NP - 1)], loss_send.at[1 + v])
+    await_bytes(dot_buf.at[pl.ds(0, NP - 1)], loss_send.at[1])
 
 
 def finish(out, loss_in, tgt_hbm, loss_hbm, loss, sem, loss_sem):
@@ -310,7 +312,7 @@
             pltpu.VMEM((ITERS, NB, CB, 128), F32),
             pltpu.VMEM((ITERS, NP, RB, 128), F32),
             pltpu.VMEM((NP, VIEWS, RB, 128), F32),
-            pltpu.VMEM((VIEWS, NP, RB, 128), F32),
+            pltpu.VMEM((NP, VIEWS * RB, 128), BF16),
             dma((2,)),
             dma((STU_CHUNKS,)),
             dma,
@@ -323,8 +325,8 @@
             dma((ITERS,)),
             dma((ITERS,)),
             dma((ITERS,)),
-            dma((1 + VIEWS,)),
-            dma((1 + VIEWS,)),
+            dma((2,)),
+            dma((2,)),
         ],
         compiler_params=pltpu.CompilerParams(
             collective_id=0, has_side_effects=True, vmem_limit_bytes=VMEM_LIMIT

time: 64.5 us -> 61 us (0.946)
  Pallas kernels: 63.8 us -> 60.3 us
    pallas_call x1, Pallas kernels: 61.7 us -> 58.2 us  [local(): pl.pallas_call(kernel, out_shape=(jax.ShapeDtypeStruct((ROWS, COLS), BF16...]
where the time goes in v3:
time: 61 us; the launch traced here: 60.9 us
  Pallas kernels  60.3 us (99%)
  between operations  0.64 us (1%)
    pallas_call x1, Pallas kernels, local(): pl.pallas_call(kernel, out_shape=(jax.ShapeDtypeStruct((ROWS, COLS), BF16...  58.2 us
    pallas_call x1, Pallas kernels, local(): pl.pallas_call(finish, out_shape=(jax.ShapeDtypeStruct((ROWS, COLS), BF16...  2.08 us

profile of v3, /device:TPU:1, one launch (start us, length us, event | category | flops | bytes accessed | tf_op | source)
XLA Modules:
  0.0 60.9 jit_solution(17940585237530429420)
XLA Ops:
  0.6 58.2 %shard_map.50 = (bf16[1024,2048]{1,0:T(8,128)(2,1)S(1)}, f32[2,8,128]{2,1,0:T(8,128)S(1)}) custom-call(bf16[32,256]{1,0:T(8,128)(2,1)} %feat_ref.1, bf16[32,2048]{1,0:T(8,128)(2,1)} %head_ref.1, bf16[2,1024,2048]{2,1,0:T(8,128)(2,1)} %stu_hbm.1), custom_call_target="tpu_custom_call" | custom-call | tf_op jit(solution)/shard_map/pallas_call | solution.py:294
  58.9 2.1 %shard_map.51 = (bf16[1024,2048]{1,0:T(8,128)(2,1)}, f32[2,1024]{1,0:T(2,128)}) custom-call(bf16[1024,2048]{1,0:T(8,128)(2,1)S(1)} %get-tuple-element.4.out, f32[2,8,128]{2,1,0:T(8,128)S(1)} %get-tuple-element.5.loss_in), custom_call_target="tpu_custom_call" | custom-call | tf_op jit(solution)/shard_map/pallas_call | solution.py:335

commit v4 on v3

--- a/solution.py
+++ b/solution.py
@@ -58,7 +58,7 @@
     feat_ref, head_ref, stu_hbm,
     out, loss_ref,
     feat, head, stu, balance, r_rep, part, wide, colacc, inv_w,
-    col_buf, row_buf, exp_buf, dot_buf,
+    col_buf, row_buf, last_buf, exp_buf, dot_buf,
     own_sem, stu_sem, f_send, fz_recv, fx_recv, w_send, wy_recv, wc_recv,
     col_send, col_recv, row_send, row_recv, loss_send, loss_recv,
 ):
@@ -177,9 +177,9 @@
             remote(mine, mine, send, recv, proto_at(dx, dz))
 
     def total(buf, n):
-        acc = buf[0]
+        acc = buf[0].astype(F32)
         for k in range(1, n):
-            acc = acc + buf[k]
+            acc = acc + buf[k].astype(F32)
         return acc
 
     for step in range(ITERS):
@@ -211,9 +211,10 @@
             return carry
 
         lax.fori_loop(0, ROWS // 128, row_rows, 0)
-        mine = row_buf.at[step, p]
+        rows_buf = last_buf if step == ITERS - 1 else row_buf.at[step]
+        mine = rows_buf.at[p]
         own_sums = lane_sums(lambda a: part[a * 128 : (a + 1) * 128, :])
-        mine[...] = own_sums
+        mine[...] = own_sums.astype(rows_buf.dtype)
         send_rows(mine, row_buf, row_send.at[step], row_recv.at[step])
         if step == 0:
             exp_sums()
@@ -243,8 +244,8 @@
             mine = dot_buf.at[p]
             mine[...] = jnp.concatenate(losses, axis=0).astype(BF16)
             send_rows(mine, dot_buf, loss_send.at[1], loss_recv.at[1])
-        await_bytes(row_buf.at[step, pl.ds(0, NP - 1)], row_recv.at[step])
-        row_inv = 1.0 / total(row_buf.at[step], NP)
+        await_bytes(rows_buf.at[pl.ds(0, NP - 1)], row_recv.at[step])
+        row_inv = 1.0 / total(rows_buf, NP)
         for a in range(RB):
             r_rep[a * 128 : (a + 1) * 128, :] = jnp.broadcast_to(row_inv[a : a + 1, :], (128, 128)).T
 
@@ -268,7 +269,8 @@
     await_bytes(head.at[pl.ds(0, (NB - 1) * WCH), :], w_send)
     for step in range(ITERS):
         await_bytes(col_buf.at[step, pl.ds(0, NB - 1)], col_send.at[step])
-        await_bytes(row_buf.at[step, pl.ds(0, NP - 1)], row_send.at[step])
+        rows_buf = last_buf if step == ITERS - 1 else row_buf.at[step]
+        await_bytes(rows_buf.at[pl.ds(0, NP - 1)], row_send.at[step])
     await_bytes(exp_buf.at[pl.ds(0, NP - 1)], loss_send.at[0])
     await_bytes(dot_buf.at[pl.ds(0, NP - 1)], loss_send.at[1])
 
@@ -310,7 +312,8 @@
             pltpu.VMEM((8, COLS), F32),
             pltpu.VMEM((1, COLS), F32),
             pltpu.VMEM((ITERS, NB, CB, 128), F32),
-            pltpu.VMEM((ITERS, NP, RB, 128), F32),
+            pltpu.VMEM((ITERS - 1, NP, RB, 128), BF16),
+            pltpu.VMEM((NP, RB, 128), F32),
             pltpu.VMEM((NP, VIEWS, RB, 128), F32),
             pltpu.VMEM((NP, VIEWS * RB, 128), BF16),
             dma((2,)),

time: 61 us -> 59.1 us (0.969)
  Pallas kernels: 60.3 us -> 58.4 us
    pallas_call x1, Pallas kernels: 58.2 us -> 56.3 us  [local(): pl.pallas_call(kernel, out_shape=(jax.ShapeDtypeStruct((ROWS, COLS), BF16...]
where the time goes in v4:
time: 59.1 us; the launch traced here: 59 us
  Pallas kernels  58.4 us (99%)
  between operations  0.64 us (1%)
    pallas_call x1, Pallas kernels, local(): pl.pallas_call(kernel, out_shape=(jax.ShapeDtypeStruct((ROWS, COLS), BF16...  56.3 us
    pallas_call x1, Pallas kernels, local(): pl.pallas_call(finish, out_shape=(jax.ShapeDtypeStruct((ROWS, COLS), BF16...  2.08 us

profile of v4, /device:TPU:1, one launch (start us, length us, event | category | flops | bytes accessed | tf_op | source)
XLA Modules:
  0.0 59.0 jit_solution(1508653029028817736)
XLA Ops:
  0.6 56.3 %shard_map.50 = (bf16[1024,2048]{1,0:T(8,128)(2,1)S(1)}, f32[2,8,128]{2,1,0:T(8,128)S(1)}) custom-call(bf16[32,256]{1,0:T(8,128)(2,1)} %feat_ref.1, bf16[32,2048]{1,0:T(8,128)(2,1)} %head_ref.1, bf16[2,1024,2048]{2,1,0:T(8,128)(2,1)} %stu_hbm.1), custom_call_target="tpu_custom_call" | custom-call | tf_op jit(solution)/shard_map/pallas_call | solution.py:296
  57.0 2.1 %shard_map.51 = (bf16[1024,2048]{1,0:T(8,128)(2,1)}, f32[2,1024]{1,0:T(2,128)}) custom-call(bf16[1024,2048]{1,0:T(8,128)(2,1)S(1)} %get-tuple-element.4.out, f32[2,8,128]{2,1,0:T(8,128)S(1)} %get-tuple-element.5.loss_in), custom_call_target="tpu_custom_call" | custom-call | tf_op jit(solution)/shard_map/pallas_call | solution.py:338
